TPU v7x, 32 devices: a whole 2x2x4 slice. The times are simulated.
32 devices in a mesh: stn: 8 (over z, y), grid: 4 (over x, core).
Axes of the slice: x: 2, y: 2, z: 4, core: 2. Of those that a mesh axis runs over, the one named last changes fastest.
Arguments:
- voltages: bfloat16 [512, 2, 12288], P('stn', None, 'grid'), may hold values from -6 to 6
- pfb_coeffs: float32 [16, 48], replicated, may hold values from -1.5 to 1.5
- station_offsets: int32 [2, 512], replicated, may hold values from 0 to 4
- tile_cells: int32 [24, 2, 136], P('stn'), may hold values from 0 to 127, as said below
- kernel_table: float32 [8, 7], replicated, may hold values from 0.2 to 1
Outputs:
- uv_grid: float32 [128, 24, 256], P('grid', 'stn')
Inputs may be any that keep to these rules, and one draw needn't show every extreme that they name: tile_cells[c, 0, k] lies in one of the strips of 32 rows; in every channel at most 68 baseline tiles have their base row in the same strip, and one strip holds exactly 68. A base row in the last strip and every base column are at most 112.
All inputs are finite; a program needn't handle non-finite values.
Results may differ from a plain program's by a relative error of at most 0.0065.
Values may be sent and summed in bfloat16 or wider, within the bound.
A program may use at most 128 MiB of HBM per device.

v0:
```python
import math
import jax
import jax.numpy as jnp
import numpy as np
from jax import lax
from jax.sharding import PartitionSpec as P

TILE = 32
PATCH = 16
SPREAD = 5
UV = 128
highest = lax.Precision.HIGHEST


def shifted(block, axis, distance):
    devices = range(lax.axis_size(axis))
    route = [(i - distance, i) for i in devices if i - distance in devices]
    return lax.ppermute(block, axis, route)


def dft_table(frame_len):
    chan_count = frame_len // 2
    sample_line = jnp.arange(frame_len, dtype=jnp.int32)[:, None]
    chan_line = jnp.arange(chan_count, dtype=jnp.int32)[None, :]
    angles = (sample_line * chan_line % frame_len).astype(jnp.float32) * (2.0 * math.pi / frame_len)
    norm_factor = 1.0 / math.sqrt(frame_len)
    twiddle = jnp.stack([jnp.cos(angles) * norm_factor, -jnp.sin(angles) * norm_factor], axis=2)
    return twiddle.reshape(frame_len, 2 * chan_count).astype(jnp.bfloat16)


CLASSES = 32
high = lax.Precision.HIGH


def fused_filter(coeffs, twiddle, step):
    taps, frame_len = coeffs.shape
    flat = coeffs.reshape(-1)
    columns = [
        jnp.pad(flat, (frame_len * (f + 1), frame_len * (step - 1 - f))) for f in range(step)
    ]
    shifted_coeffs = jnp.stack(columns, axis=0)
    spread = np.kron(np.ones((1, frame_len), np.float32), np.eye(step, dtype=np.float32))
    wide = jnp.einsum("fm,fn->mn", shifted_coeffs, jnp.asarray(spread), precision=highest)
    tiled = jnp.tile(jnp.repeat(twiddle.astype(jnp.float32), step, axis=1), (step + taps, 1))
    return (wide * tiled).astype(jnp.bfloat16)


def separation_table(frequency, divisor, kernel_table):
    over_count = kernel_table.shape[0]
    separation = jnp.arange(2 * SPREAD - 1, dtype=jnp.int32)
    scaled = separation * frequency
    cell_index = scaled // divisor
    fine_index = scaled % divisor * over_count // divisor
    choose = (fine_index[:, None] == jnp.arange(over_count, dtype=jnp.int32)[None, :]).astype(
        jnp.float32
    )
    tap_values = jnp.dot(choose, kernel_table, precision=highest)
    place_rel = jnp.arange(PATCH, dtype=jnp.int32)[None, :] - cell_index[:, None]
    weights = jnp.zeros(place_rel.shape, jnp.float32)
    for tap_index in range(kernel_table.shape[1]):
        weights = weights + tap_values[:, tap_index : tap_index + 1] * (
            place_rel == tap_index
        ).astype(jnp.float32)
    return weights


def joint_weights(frequencies, divisor, kernel_table):
    class_line = np.arange(CLASSES)
    class_u = np.minimum(class_line // SPREAD, SPREAD - 1)
    class_v = class_line % SPREAD
    sep_line = np.arange(2 * SPREAD - 1)
    pick_u = (class_u[:, None] - class_u[None, :] + SPREAD - 1).reshape(-1, 1) == sep_line
    pick_v = (class_v[:, None] - class_v[None, :] + SPREAD - 1).reshape(-1, 1) == sep_line
    weights = jnp.stack([separation_table(f, divisor, kernel_table) for f in frequencies])
    over_r = np.kron(np.eye(PATCH), np.ones((1, PATCH))).astype(np.float32)
    over_t = np.kron(np.ones((1, PATCH)), np.eye(PATCH)).astype(np.float32)
    wide_u = jnp.einsum("czr,rm->czm", weights, jnp.asarray(over_r), precision=highest)
    wide_v = jnp.einsum("czr,rm->czm", weights, jnp.asarray(over_t), precision=highest)
    full_u = jnp.einsum(
        "qz,czm->cqm", jnp.asarray(pick_u.astype(np.float32)), wide_u, precision=highest
    )
    full_v = jnp.einsum(
        "qz,czm->cqm", jnp.asarray(pick_v.astype(np.float32)), wide_v, precision=highest
    )
    return full_u * full_v


def body(voltages, pfb_coeffs, station_offsets, tile_cells, kernel_table):
    stn_local, pol_count, samples = voltages.shape
    tap_count, frame_len = pfb_coeffs.shape
    spec_count = samples // frame_len
    step = 128 // math.gcd(128, frame_len)
    chunks = spec_count // step
    flat = voltages.reshape(stn_local * pol_count, samples)
    earlier = shifted(flat[:, samples - tap_count * frame_len :], "grid", 1)
    extended = jnp.concatenate([earlier, flat], axis=1)
    width = step * frame_len
    reach = (step + tap_count) * frame_len
    blocks = jnp.stack([extended[:, c * width : c * width + reach] for c in range(chunks)], axis=1)
    matrix = fused_filter(pfb_coeffs, dft_table(frame_len), step)
    spectra = jnp.einsum("rcm,mn->nrc", blocks, matrix, preferred_element_type=jnp.float32).astype(
        jnp.bfloat16
    )
    spectra = spectra.reshape(frame_len // 2, 2, step, stn_local, pol_count * chunks)
    spectra = jnp.transpose(spectra, (0, 1, 3, 2, 4)).reshape(
        frame_len // 2, 2, stn_local, step * pol_count * chunks
    )
    turned = lax.all_to_all(spectra, "stn", split_axis=0, concat_axis=2, tiled=True)
    ch_dev, _, stations, depth = turned.shape
    tiles = stations // TILE
    divisor = frame_len - 1
    first_chan = lax.axis_index("stn") * ch_dev + frame_len // 2
    norm_factor = 1.0 / (pol_count * spec_count * lax.axis_size("grid"))
    classes = (station_offsets[0] * SPREAD + station_offsets[1]).reshape(tiles, TILE)
    hot = classes[:, :, None] == jnp.arange(CLASSES, dtype=jnp.int32)
    hot_low = hot.astype(jnp.bfloat16)
    hot_full = hot.astype(jnp.float32)
    tiled = turned.reshape(ch_dev, 2, tiles, TILE, depth)
    summed = jnp.einsum(
        "aiq,ceaik->ceaqk", hot_low, tiled, preferred_element_type=jnp.float32
    ).astype(jnp.bfloat16)

    def stacked(z):
        real_part, imag_part = (z[:, 0], z[:, 1])
        partner = jnp.concatenate([real_part, imag_part], axis=-1)
        turned_partner = jnp.concatenate([imag_part, -real_part], axis=-1)
        return (jnp.stack([partner, turned_partner], axis=1), partner)

    left, right = stacked(summed)
    cross = jnp.einsum("ceaqk,cbsk->ceabqs", left, right, preferred_element_type=jnp.float32)
    joint = joint_weights([first_chan + i for i in range(ch_dev)], divisor, kernel_table)
    joint = joint * norm_factor
    patch = jnp.einsum(
        "ceabm,cmn->ceabn",
        cross.reshape(ch_dev, 2, tiles, tiles, CLASSES * CLASSES),
        joint,
        precision=high,
    )
    own_left, own_right = stacked(tiled)
    own = jnp.einsum("ceaik,cajk->ceaij", own_left, own_right, preferred_element_type=jnp.float32)
    line = np.arange(TILE)
    own = jnp.where(jnp.asarray(line[:, None] < line[None, :]), own, 0.0)
    own = jnp.einsum("aiq,ceaij->ceaqj", hot_full, own, precision=high)
    own = jnp.einsum("ceaqj,ajs->ceaqs", own, hot_full, precision=high)
    own_patch = jnp.einsum(
        "ceam,cmn->cean", own.reshape(ch_dev, 2, tiles, CLASSES * CLASSES), joint, precision=high
    )
    same = np.eye(tiles, dtype=bool)[:, :, None]
    patch = jnp.where(jnp.asarray(same), own_patch[:, :, :, None, :], patch)
    pair_first, pair_second = np.triu_indices(tiles)
    select = np.zeros((pair_first.size, tiles * tiles), np.float32)
    select[np.arange(pair_first.size), pair_first * tiles + pair_second] = 1.0
    missing = (1.0 - select.sum(axis=0)).astype(np.int32) * 4096
    cells = jnp.einsum(
        "cxk,kp->cxp", tile_cells.astype(jnp.float32), jnp.asarray(select), precision=highest
    )
    cells = jnp.round(cells).astype(jnp.int32) + jnp.asarray(missing)
    patch = patch.reshape(ch_dev, 2, tiles * tiles, PATCH, PATCH)
    patch_line = jnp.arange(PATCH, dtype=jnp.int32)
    target = cells[..., None] + patch_line
    spots = (target[..., None] == jnp.arange(UV, dtype=jnp.int32)).astype(jnp.float32)
    rows, cols = (spots[:, 0], spots[:, 1])
    spread_cols = jnp.einsum("cekrt,cktw->ckrew", patch, cols, precision=high)
    planes = jnp.einsum("ckru,ckrew->ucew", rows, spread_cols, precision=high)
    planes = planes.reshape(UV, ch_dev, 2 * UV)
    return lax.psum_scatter(planes, "grid", scatter_dimension=0, tiled=True)


def solution(mesh):
    placed = (P("stn", None, "grid"), P(), P(), P("stn", None, None), P())
    return jax.shard_map(
        body, mesh=mesh, in_specs=placed, out_specs=P("grid", "stn", None), check_vma=False
    )
```

profile of v0, /device:TPU:0, one launch (start us, length us, event | category | flops | bytes accessed | tf_op | source)
XLA Modules:
  0.0 228.6 jit_solution(5774973549644276165)
XLA Ops:
  6.5 2.3 %reshape.1055 = bf16[128,3072]{1,0:T(8,128)(2,1)S(1)} reshape(bf16[64,2,3072]{2,1,0:T(2,128)(2,1)} %param.14) | data formatting | bytes 1572864 | tf_op jit(solution)/shard_map/reshape | solution.py:94
  8.9 2.4 %collective-permute-start = (bf16[128,768]{1,0:T(8,128)(2,1)S(1)}, bf16[128,768]{1,0:T(8,128)(2,1)S(1)}, u32[]{:S(2)}, u32[]{:S(2)}) collective-permute-start(bf16[128,768]{1,0:T(8,128)(2,1)S(1)} %slice.161), channel_id=1, source_target_pairs={{0,1},{1,2},{2,3},{4,5},{5,6},{6,7},{8,9},{9,10},{10,11},{12,13},{... | collective-permute-start | bytes 589832 | tf_op jit(solution)/shard_map/ppermute | solution.py:18
  13.1 4.3 %fusion.99 = f32[3,256,1024]{2,1,0:T(8,128)} fusion(f32[3,9,256]{2,1,0:T(8,128)S(1)} %fusion.53, f32[1024,9,1]{0,1,2:T(8,128)S(1)} %copy-done.7), kind=kOutput, calls=%fused_computation.178 | convolution fusion | flops 84934656 | bytes 3210240 | tf_op jit(solution)/shard_map/qz,czm->cqm/dot_general | solution.py:79
  17.7 1.3 fusion.8
  19.5 1.2 convolution_convert_fusion.1
  20.8 0.5 copy.103
  21.3 15.6 %reshape.1056 = bf16[24,2,8,64,16]{2,1,0,4,3:T(2,128)(2,1)} reshape(bf16[384,128,8]{0,2,1:T(8,128)(2,1)S(1)} %copy.103) | data formatting | bytes 1572864 | tf_op jit(solution)/shard_map/reshape | solution.py:104
  37.0 30.5 %copy.104 = bf16[24,2,64,8,16]{2,4,3,1,0:T(8,128)(2,1)S(1)} copy(bf16[24,2,64,8,16]{3,1,0,4,2:T(2,128)(2,1)} %bitcast.218) | data formatting | bytes 1572864 | tf_op jit(solution)/shard_map/transpose | solution.py:105
  67.5 1.4 copy.105
  68.9 6.8 %all-to-all-start = ((bf16[24,2,64,128]{3,2,1,0:T(8,128)(2,1)}), bf16[24,2,64,128]{3,2,1,0:T(8,128)(2,1)}, u32[]{:S(2)}, u32[]{:S(2)}) async-start(bf16[24,2,64,128]{3,2,1,0:T(8,128)(2,1)} %copy.105), calls=%async_computation | async-start | bytes 1572864 | tf_op jit(solution)/shard_map/all_to_all | solution.py:108
  76.3 4.7 %multiply_multiply_fusion = f32[3,256,1024]{2,1,0:T(8,128)S(1)} fusion(f32[3,256,1024]{2,1,0:T(8,128)} %fusion.99, f32[3,9,256]{2,1,0:T(8,128)S(1)} %fusion.52, f32[1024,9,1]{0,1,2:T(8,128)S(1)} %copy-done.6), kind=kOutput, calls=%fused_computation.12 | convolution fusion | flops 86507520 | bytes 6355968 | tf_op jit(solution)/shard_map/qz,czm->cqm/dot_general | solution.py:82
  81.1 5.4 %iota_compare_fusion = pred[3,2,256,16,128]{4,3,2,0,1:T(8,128)(4,1)} fusion(s32[3,2,256,16]{3,2,0,1:T(8,128)S(1)} %iota_add_fusion), kind=kLoop, calls=%fused_computation.4 | loop fusion | flops 3145728 | bytes 3244032 | tf_op jit(solution)/shard_map/eq | solution.py:161
  86.5 10.8 %all-to-all-done = bf16[24,2,64,128]{3,2,1,0:T(8,128)(2,1)} async-done(((bf16[24,2,64,128]{3,2,1,0:T(8,128)(2,1)}), bf16[24,2,64,128]{3,2,1,0:T(8,128)(2,1)}, u32[]{:S(2)}, u32[]{:S(2)}) %all-to-all-start) | async-done | bytes 786464 | tf_op jit(solution)/shard_map/all_to_all | solution.py:108
  97.3 1.2 copy.106
  98.5 0.4 fusion.26
  99.0 1.0 slice_bitcast_fusion.7
  100.3 10.1 %convolution_bitcast_fusion = f32[3,2,16,16,32,32]{4,5,2,1,3,0:T(8,128)} fusion(bf16[3,16,32,256,1,1]{3,2,0,1,5,4:T(8,128)(2,1)S(1)} %get-tuple-element.7, bf16[3,1,16,32,256]{4,3,0,2,1:T(8,128)(2,1)S(1)} %get-tuple-element.13, bf16[3,1,16,32,256]{4,3,0,2,1:T(8,128)(2,1)S(1)} %get-tuple-element.8), kind=kOutput, calls=%fused_computation.5 | convolution fusion | flops 806092800 | bytes 8650752 | tf_op jit(solution)/shard_map/ceaqk,cbsk->ceabqs/dot_general | solution.py:130
  110.4 24.9 %copy.118 = f32[3,2,16,16,32,32]{5,4,3,2,1,0:T(8,128)} copy(f32[3,2,16,16,32,32]{4,5,2,1,3,0:T(8,128)} %convolution_bitcast_fusion) | data formatting | bytes 12582912 | tf_op jit(solution)/shard_map/ceaqk,cbsk->ceabqs/transpose | solution.py:130
  135.3 19.9 %reshape.1060 = f32[3,2,16,16,1024]{4,3,2,1,0:T(8,128)} reshape(f32[3,2,16,16,32,32]{5,4,3,2,1,0:T(8,128)} %copy.118) | data formatting | bytes 12582912 | tf_op jit(solution)/shard_map/reshape | solution.py:135
  155.3 1.6 fusion.36
  156.9 1.3 bitcast_select_fusion
  158.2 0.6 fusion.16
  158.8 1.7 fusion.18
  160.6 3.0 %copy.113 = f32[3,2,16,32,32]{4,3,2,1,0:T(8,128)} copy(f32[3,2,16,32,32]{3,4,1,0,2:T(8,128)} %fusion.18) | data formatting | bytes 786432 | tf_op jit(solution)/shard_map/ceaqj,ajs->ceaqs/transpose | solution.py:144
  163.6 2.1 reshape.1059
  165.7 1.5 fusion.6
  167.3 6.8 %fusion.23 = f32[3,2,16,16,256]{4,3,2,1,0:T(8,128)} fusion(f32[3,2,16,16,1024]{4,3,2,1,0:T(8,128)} %reshape.1060, f32[3,256,1024]{2,1,0:T(8,128)S(1)} %multiply_multiply_fusion, f32[3,2,16,256]{3,2,1,0:T(8,128)S(1)} %fusion.6, pred[16,16]{1,0:T(8,128)(4,1)S(1)} %copy-done.11), kind=kOutput, calls=%fused_computation.34 | convolution fusion | flops 2416312320 | bytes 11108608 | tf_op jit(solution)/shard_map/ceabm,cmn->ceabn/dot_general | solution.py:133
  174.1 8.4 %reshape.1061 = f32[3,2,256,16,16]{4,3,2,1,0:T(8,128)} reshape(f32[3,2,16,16,256]{4,3,2,1,0:T(8,128)} %fusion.23) | data formatting | bytes 3145728 | tf_op jit(solution)/shard_map/reshape | solution.py:158
  182.5 9.3 %fusion.2 = f32[3,256,128,2,16]{2,4,3,1,0:T(8,128)} fusion(f32[3,2,256,16,16]{4,3,2,1,0:T(8,128)} %reshape.1061, pred[3,2,256,16,128]{4,3,2,0,1:T(8,128)(4,1)S(1)} %copy-done.2), kind=kOutput, calls=%fused_computation.2 | convolution fusion | flops 301989888 | bytes 15728640 | tf_op jit(solution)/shard_map/cekrt,cktw->ckrew/dot_general | solution.py:163
  191.8 9.8 %fusion = f32[3,2,128,128,1]{3,2,1,4,0:T(8,128)S(1)} fusion(f32[3,256,128,2,16]{2,4,3,1,0:T(8,128)} %fusion.2, pred[3,2,256,16,128]{4,3,2,0,1:T(8,128)(4,1)S(1)} %copy-done.2), kind=kOutput, calls=%fused_computation | convolution fusion | flops 2415919104 | bytes 14548992 | tf_op jit(solution)/shard_map/ckru,ckrew->ucew/dot_general | solution.py:164
  201.7 0.9 copy.121
  202.6 19.1 %reduce-scatter.2.cloned.1.call-done = f32[32,3,256]{2,0,1:T(8,128)} async-done(((f32[128,3,256]{2,0,1:T(8,128)}), f32[32,3,256]{2,0,1:T(8,128)}) %reduce-scatter.2.cloned.1.call-update) | async-done | bytes 98320 | tf_op jit(solution)/shard_map/reduce_scatter | solution.py:166
  (92 shorter events, 3.4 us)
Async XLA Ops:
  6.5 5.2 %copy-start = (f32[8,7]{1,0:T(8,128)S(1)}, f32[8,7]{1,0:T(8,128)}, u32[]{:S(2)}) copy-start(f32[8,7]{1,0:T(8,128)} %param.18) | copy-start | bytes 676
  6.5 6.3 %copy-start.9 = (f32[16,256,1]{1,0,2:T(8,128)S(1)}, f32[16,256,1]{1,0,2:T(8,128)}, u32[]{:S(2)}) copy-start(f32[16,256,1]{1,0,2:T(8,128)} %constant.175) | copy-start | bytes 49156
  6.5 6.5 %copy-start.7 = (f32[1024,9,1]{0,1,2:T(8,128)S(1)}, f32[1024,9,1]{0,1,2:T(8,128)}, u32[]{:S(2)}) copy-start(f32[1024,9,1]{0,1,2:T(8,128)} %constant.176) | copy-start | bytes 110596
  6.5 4.8 %copy-start.10 = (f32[16,48]{1,0:T(8,128)S(1)}, f32[16,48]{1,0:T(8,128)}, u32[]{:S(2)}) copy-start(f32[16,48]{1,0:T(8,128)} %param.15) | copy-start | bytes 9220
  6.5 5.9 %copy-start.12 = (s32[3,2,136]{2,1,0:T(2,128)S(1)}, s32[3,2,136]{2,1,0:T(2,128)}, u32[]{:S(2)}) copy-start(s32[3,2,136]{2,1,0:T(2,128)} %param.17) | copy-start | bytes 9796
  8.9 10.2 %collective-permute-start = (bf16[128,768]{1,0:T(8,128)(2,1)S(1)}, bf16[128,768]{1,0:T(8,128)(2,1)S(1)}, u32[]{:S(2)}, u32[]{:S(2)}) collective-permute-start(bf16[128,768]{1,0:T(8,128)(2,1)S(1)} %slice.161), channel_id=1, source_target_pairs={{0,1},{1,2},{2,3},{4,5},{5,6},{6,7},{8,9},{9,10},{10,11},{12,13},{... | collective-permute-start | bytes 589832 | tf_op jit(solution)/shard_map/ppermute | solution.py:18
  12.2 5.2 %copy-start.5 = (f32[136,256,1]{1,0,2:T(8,128)S(1)}, f32[136,256,1]{1,0,2:T(8,128)}, u32[]{:S(2)}) copy-start(f32[136,256,1]{1,0,2:T(8,128)} %constant.174) | copy-start | bytes 417796
  12.2 5.2 %copy-start.22 = (s32[256]{0:T(256)S(1)}, s32[256]{0:T(256)}, u32[]{:S(2)}) copy-start(s32[256]{0:T(256)} %constant.139.clone) | copy-start | bytes 3076
  12.7 4.9 %copy-start.14 = (f32[384]{0:T(512)S(1)}, f32[384]{0:T(512)}, u32[]{:S(2)}) copy-start(f32[384]{0:T(512)} %constant.173) | copy-start | bytes 4612
  12.7 4.9 %copy-start.15 = (f32[384]{0:T(512)S(1)}, f32[384]{0:T(512)}, u32[]{:S(2)}) copy-start(f32[384]{0:T(512)} %constant.171) | copy-start | bytes 4612
  12.7 4.9 %copy-start.16 = (f32[384]{0:T(512)S(1)}, f32[384]{0:T(512)}, u32[]{:S(2)}) copy-start(f32[384]{0:T(512)} %constant.169) | copy-start | bytes 4612
  12.7 4.9 %copy-start.17 = (f32[384]{0:T(512)S(1)}, f32[384]{0:T(512)}, u32[]{:S(2)}) copy-start(f32[384]{0:T(512)} %constant.167) | copy-start | bytes 4612
  12.7 4.9 %copy-start.18 = (f32[384]{0:T(512)S(1)}, f32[384]{0:T(512)}, u32[]{:S(2)}) copy-start(f32[384]{0:T(512)} %constant.165) | copy-start | bytes 4612
  12.7 4.9 %copy-start.19 = (f32[384]{0:T(512)S(1)}, f32[384]{0:T(512)}, u32[]{:S(2)}) copy-start(f32[384]{0:T(512)} %constant.163) | copy-start | bytes 4612
  12.7 4.9 %copy-start.20 = (f32[384]{0:T(512)S(1)}, f32[384]{0:T(512)}, u32[]{:S(2)}) copy-start(f32[384]{0:T(512)} %constant.161) | copy-start | bytes 4612
  12.8 4.9 %copy-start.21 = (f32[384]{0:T(512)S(1)}, f32[384]{0:T(512)}, u32[]{:S(2)}) copy-start(f32[384]{0:T(512)} %constant.159) | copy-start | bytes 4612
  13.1 5.9 %copy-start.8 = (f32[16,256,1]{1,0,2:T(8,128)S(1)}, f32[16,256,1]{1,0,2:T(8,128)}, u32[]{:S(2)}) copy-start(f32[16,256,1]{1,0,2:T(8,128)} %constant.177) | copy-start | bytes 49156
  67.5 8.4 %copy-start.13 = (s32[2,512]{1,0:T(2,128)S(1)}, s32[2,512]{1,0:T(2,128)}, u32[]{:S(2)}) copy-start(s32[2,512]{1,0:T(2,128)} %param.16) | copy-start | bytes 12292
  68.9 7.4 %copy-start.6 = (f32[1024,9,1]{0,1,2:T(8,128)S(1)}, f32[1024,9,1]{0,1,2:T(8,128)}, u32[]{:S(2)}) copy-start(f32[1024,9,1]{0,1,2:T(8,128)} %constant.178) | copy-start | bytes 110596
  68.9 28.4 %all-to-all-start = ((bf16[24,2,64,128]{3,2,1,0:T(8,128)(2,1)}), bf16[24,2,64,128]{3,2,1,0:T(8,128)(2,1)}, u32[]{:S(2)}, u32[]{:S(2)}) async-start(bf16[24,2,64,128]{3,2,1,0:T(8,128)(2,1)} %copy.105), calls=%async_computation | async-start | bytes 1572864 | tf_op jit(solution)/shard_map/all_to_all | solution.py:108
  75.7 146.0 %reduce-scatter.2.cloned.1.call-start = ((), (), s32[]{:S(2)}) async-start(), calls=%async_computation.2 | async-start | bytes 491520 | tf_op jit(solution)/shard_map/reduce_scatter | solution.py:166
  155.3 1.6 copy-start.3
  155.3 1.6 copy-start.4
  155.3 1.7 copy-start.23
  165.7 1.6 copy-start.11
  174.1 8.4 %copy-start.2 = (pred[3,2,256,16,128]{4,3,2,0,1:T(8,128)(4,1)S(1)}, pred[3,2,256,16,128]{4,3,2,0,1:T(8,128)(4,1)}, u32[]{:S(2)}) copy-start(pred[3,2,256,16,128]{4,3,2,0,1:T(8,128)(4,1)} %iota_compare_fusion) | copy-start | bytes 9437188
  191.8 29.9 %copy-start.1 = (f32[8,7]{1,0:T(8,128)S(1)}, f32[8,7]{1,0:T(8,128)}, u32[]{:S(2)}) copy-start(f32[8,7]{1,0:T(8,128)} %param.18) | copy-start | bytes 676
Sparse Core Ops, SparseCore 0:
  202.7 18.9 reduce-scatter.1
where the time goes:
time: 230 us; the launch traced here: 229 us
  local copies, waits for them, and re-layouts  113 us (49%)
  matrix products  53 us (23%)
  waiting for transfers between devices  30 us (13%)
  between operations  14 us (6%)
  other arithmetic  9.47 us (4%)
  starting transfers between devices  9.38 us (4%)
    transpose x1, local copies, waits for them, and re-layouts, body(): jnp.transpose(spectra, (0, 1, 3, 2, 4))  30.5 us
    transpose x1, local copies, waits for them, and re-layouts, body(): jnp.einsum('ceaqk,cbsk->ceabqs', left, right, preferred_element_type=jnp....  24.9 us
    reshape x1, local copies, waits for them, and re-layouts, body(): cross.reshape(ch_dev, 2, tiles, tiles, CLASSES * CLASSES)  19.9 us
    reduce_scatter x1, waiting for transfers between devices, body(): return lax.psum_scatter(planes, 'grid', scatter_dimension=0, tiled=True)  19.1 us
    reshape x1, local copies, waits for them, and re-layouts, body(): spectra.reshape(frame_len // 2, 2, step, stn_local, pol_count * chunks)  15.6 us
    all_to_all x1, waiting for transfers between devices, body(): lax.all_to_all(spectra, 'stn', split_axis=0, concat_axis=2, tiled=True)  10.8 us
    dot_general x1, matrix products, body(): jnp.einsum('ceaqk,cbsk->ceabqs', left, right, preferred_element_type=jnp....  10.1 us
    dot_general x1, matrix products, body(): planes = jnp.einsum('ckru,ckrew->ucew', rows, spread_cols, precision=high)  9.85 us
  transfers between devices with their start and end apart: 3, of which 2 were waited for; matrix products, arithmetic and copies ran while one was open for 8% of the time, Pallas kernels for 0%

commit v1 on v0

--- a/solution.py
+++ b/solution.py
@@ -105,7 +105,10 @@
     spectra = jnp.transpose(spectra, (0, 1, 3, 2, 4)).reshape(
         frame_len // 2, 2, stn_local, step * pol_count * chunks
     )
-    turned = lax.all_to_all(spectra, "stn", split_axis=0, concat_axis=2, tiled=True)
+    turned = jnp.concatenate(
+        lax.all_to_all(jnp.stack(jnp.split(spectra, lax.axis_size("stn"), axis=0)), "stn", 0, 0),
+        axis=2,
+    )
     ch_dev, _, stations, depth = turned.shape
     tiles = stations // TILE
     divisor = frame_len - 1

time: 230 us -> 254 us (1.10)
  local copies, waits for them, and re-layouts: 113 us -> 135 us
    split x0 -> x9, local copies, waits for them, and re-layouts: none -> 47 us  [body(): jnp.split(spectra, lax.axis_size('stn'), axis=0)]
    transpose x1 -> x0, local copies, waits for them, and re-layouts: 30.5 us -> none  [body(): jnp.transpose(spectra, (0, 1, 3, 2, 4))]
    unnamed x56 -> x69, local copies, waits for them, and re-layouts: 0.37 us -> 5.88 us
where the time goes in v1:
time: 254 us; the launch traced here: 252 us
  local copies, waits for them, and re-layouts  135 us (53%)
  matrix products  54.2 us (21%)
  waiting for transfers between devices  29.9 us (12%)
  between operations  14 us (6%)
  other arithmetic  9.45 us (4%)
  starting transfers between devices  9.38 us (4%)
    split x9, local copies, waits for them, and re-layouts, body(): jnp.split(spectra, lax.axis_size('stn'), axis=0)  47 us
    transpose x1, local copies, waits for them, and re-layouts, body(): jnp.einsum('ceaqk,cbsk->ceabqs', left, right, preferred_element_type=jnp....  24.9 us
    reshape x1, local copies, waits for them, and re-layouts, body(): cross.reshape(ch_dev, 2, tiles, tiles, CLASSES * CLASSES)  19.9 us
    reduce_scatter x1, waiting for transfers between devices, body(): return lax.psum_scatter(planes, 'grid', scatter_dimension=0, tiled=True)  19.1 us
    reshape x1, local copies, waits for them, and re-layouts, body(): spectra.reshape(frame_len // 2, 2, step, stn_local, pol_count * chunks)  15.6 us
    all_to_all x1, waiting for transfers between devices, body(): lax.all_to_all(jnp.stack(jnp.split(spectra, lax.axis_size('stn'), axis=0)...  10.8 us
    dot_general x1, matrix products, body(): jnp.einsum('ceaqk,cbsk->ceabqs', left, right, preferred_element_type=jnp....  10.1 us
    dot_general x1, matrix products, body(): planes = jnp.einsum('ckru,ckrew->ucew', rows, spread_cols, precision=high)  9.85 us
  transfers between devices with their start and end apart: 3, of which 2 were waited for; matrix products, arithmetic and copies ran while one was open for 8% of the time, Pallas kernels for 0%

profile of v1, /device:TPU:0, one launch (start us, length us, event | category | flops | bytes accessed | tf_op | source)
XLA Modules:
  0.0 251.7 jit_solution(1560652880823462930)
XLA Ops:
  6.5 2.3 reshape.1068
  8.9 2.4 collective-permute-start
  13.1 4.3 %fusion.100 = f32[3,256,1024]{2,1,0:T(8,128)} fusion(f32[3,9,256]{2,1,0:T(8,128)S(1)} %fusion.53, f32[1024,9,1]{0,1,2:T(8,128)S(1)} %copy-done.9), kind=kOutput, calls=%fused_computation.187 | convolution fusion | flops 84934656 | bytes 3210240 | tf_op jit(solution)/shard_map/qz,czm->cqm/dot_general | solution.py:79
  22.5 15.6 %reshape.1069 = bf16[24,2,8,64,16]{2,1,0,4,3:T(2,128)(2,1)} reshape(bf16[384,128,8]{0,2,1:T(8,128)(2,1)S(1)} %copy.103) | data formatting | bytes 1572864 | tf_op jit(solution)/shard_map/reshape | solution.py:104
  38.1 13.2 %fusion.98 = (bf16[3,2,64,8,16]{3,1,0,4,2:T(2,128)(2,1)S(1)}, bf16[3,2,64,8,16]{3,1,0,4,2:T(2,128)(2,1)S(1)}, bf16[3,2,64,8,16]{3,1,0,4,2:T(2,128)(2,1)}, bf16[3...) fusion(bf16[24,2,64,8,16]{3,1,0,4,2:T(2,128)(2,1)} %bitcast.224), kind=kLoop, calls=%fused_computation.185 | loop fusion | bytes 1572864 | tf_op jit(solution)/shard_map/split | solution.py:109
  51.4 4.0 %copy.104 = bf16[3,2,64,8,16]{2,4,3,1,0:T(8,128)(2,1)S(1)} copy(bf16[3,2,64,8,16]{3,1,0,4,2:T(2,128)(2,1)} %get-tuple-element.12) | data formatting | bytes 196608 | tf_op jit(solution)/shard_map/split | solution.py:109
  56.1 4.9 %copy.105 = bf16[3,2,64,8,16]{2,4,3,1,0:T(8,128)(2,1)} copy(bf16[3,2,64,8,16]{3,1,0,4,2:T(2,128)(2,1)} %get-tuple-element.11) | data formatting | bytes 196608 | tf_op jit(solution)/shard_map/split | solution.py:109
  61.0 4.9 %copy.106 = bf16[3,2,64,8,16]{2,4,3,1,0:T(8,128)(2,1)} copy(bf16[3,2,64,8,16]{3,1,0,4,2:T(2,128)(2,1)} %get-tuple-element.10) | data formatting | bytes 196608 | tf_op jit(solution)/shard_map/split | solution.py:109
  65.9 4.9 %copy.107 = bf16[3,2,64,8,16]{2,4,3,1,0:T(8,128)(2,1)} copy(bf16[3,2,64,8,16]{3,1,0,4,2:T(2,128)(2,1)} %get-tuple-element.9) | data formatting | bytes 196608 | tf_op jit(solution)/shard_map/split | solution.py:109
  70.8 4.9 %copy.108 = bf16[3,2,64,8,16]{2,4,3,1,0:T(8,128)(2,1)} copy(bf16[3,2,64,8,16]{3,1,0,4,2:T(2,128)(2,1)} %get-tuple-element.8) | data formatting | bytes 196608 | tf_op jit(solution)/shard_map/split | solution.py:109
  75.7 4.9 %copy.109 = bf16[3,2,64,8,16]{2,4,3,1,0:T(8,128)(2,1)} copy(bf16[3,2,64,8,16]{3,1,0,4,2:T(2,128)(2,1)} %get-tuple-element.7) | data formatting | bytes 196608 | tf_op jit(solution)/shard_map/split | solution.py:109
  80.6 2.6 %copy.110 = bf16[3,2,64,8,16]{2,4,3,1,0:T(8,128)(2,1)S(1)} copy(bf16[3,2,64,8,16]{3,1,0,4,2:T(2,128)(2,1)S(1)} %get-tuple-element.6) | data formatting | bytes 196608 | tf_op jit(solution)/shard_map/split | solution.py:109
  83.2 2.6 %copy.111 = bf16[3,2,64,8,16]{2,4,3,1,0:T(8,128)(2,1)S(1)} copy(bf16[3,2,64,8,16]{3,1,0,4,2:T(2,128)(2,1)S(1)} %get-tuple-element.5) | data formatting | bytes 196608 | tf_op jit(solution)/shard_map/split | solution.py:109
  90.7 1.4 copy.112
  92.2 6.8 %all-to-all-start = ((bf16[8,3,2,64,128]{4,3,2,1,0:T(8,128)(2,1)}), bf16[8,3,2,64,128]{4,3,2,1,0:T(8,128)(2,1)}, u32[]{:S(2)}, u32[]{:S(2)}) async-start(bf16[8,3,2,64,128]{4,3,2,1,0:T(8,128)(2,1)} %copy.112), calls=%async_computation | async-start | bytes 1572864 | tf_op jit(solution)/shard_map/all_to_all | solution.py:109
  99.6 4.7 %multiply_multiply_fusion = f32[3,256,1024]{2,1,0:T(8,128)S(1)} fusion(f32[3,256,1024]{2,1,0:T(8,128)} %fusion.100, f32[3,9,256]{2,1,0:T(8,128)S(1)} %copy-done.6, f32[1024,9,1]{0,1,2:T(8,128)S(1)} %copy-done.8), kind=kOutput, calls=%fused_computation.12 | convolution fusion | flops 86507520 | bytes 6355968 | tf_op jit(solution)/shard_map/qz,czm->cqm/dot_general | solution.py:82
  104.3 5.4 %iota_compare_fusion = pred[3,2,256,16,128]{4,3,2,0,1:T(8,128)(4,1)} fusion(s32[3,2,256,16]{3,2,0,1:T(8,128)S(1)} %iota_add_fusion), kind=kLoop, calls=%fused_computation.4 | loop fusion | flops 3145728 | bytes 3244032 | tf_op jit(solution)/shard_map/eq | solution.py:164
  109.7 10.8 %all-to-all-done = bf16[8,3,2,64,128]{4,3,2,1,0:T(8,128)(2,1)} async-done(((bf16[8,3,2,64,128]{4,3,2,1,0:T(8,128)(2,1)}), bf16[8,3,2,64,128]{4,3,2,1,0:T(8,128)(2,1)}, u32[]{:S(2)}, u32[]{:S(2)}) %all-to-all-start) | async-done | bytes 786464 | tf_op jit(solution)/shard_map/all_to_all | solution.py:109
  123.6 10.1 %convolution_bitcast_fusion = f32[3,2,16,16,32,32]{4,5,2,1,3,0:T(8,128)} fusion(bf16[3,16,32,256,1,1]{3,2,0,1,5,4:T(8,128)(2,1)S(1)} %get-tuple-element.15, bf16[3,1,16,32,256]{4,3,0,2,1:T(8,128)(2,1)S(1)} %get-tuple-element.21, bf16[3,1,16,32,256]{4,3,0,2,1:T(8,128)(2,1)S(1)} %get-tuple-element.16), kind=kOutput, calls=%fused_computation.5 | convolution fusion | flops 806092800 | bytes 8650752 | tf_op jit(solution)/shard_map/ceaqk,cbsk->ceabqs/dot_general | solution.py:133
  133.7 24.9 %copy.125 = f32[3,2,16,16,32,32]{5,4,3,2,1,0:T(8,128)} copy(f32[3,2,16,16,32,32]{4,5,2,1,3,0:T(8,128)} %convolution_bitcast_fusion) | data formatting | bytes 12582912 | tf_op jit(solution)/shard_map/ceaqk,cbsk->ceabqs/transpose | solution.py:133
  158.5 19.9 %reshape.1072 = f32[3,2,16,16,1024]{4,3,2,1,0:T(8,128)} reshape(f32[3,2,16,16,32,32]{5,4,3,2,1,0:T(8,128)} %copy.125) | data formatting | bytes 12582912 | tf_op jit(solution)/shard_map/reshape | solution.py:138
  178.4 1.6 fusion.36
  180.1 1.3 bitcast_select_fusion
  182.0 1.7 fusion.18
  183.7 3.0 %copy.120 = f32[3,2,16,32,32]{4,3,2,1,0:T(8,128)} copy(f32[3,2,16,32,32]{3,4,1,0,2:T(8,128)} %fusion.18) | data formatting | bytes 786432 | tf_op jit(solution)/shard_map/ceaqj,ajs->ceaqs/transpose | solution.py:147
  186.7 2.1 reshape.1071
  188.8 1.5 fusion.6
  190.4 6.8 %fusion.23 = f32[3,2,16,16,256]{4,3,2,1,0:T(8,128)} fusion(f32[3,2,16,16,1024]{4,3,2,1,0:T(8,128)} %reshape.1072, f32[3,256,1024]{2,1,0:T(8,128)S(1)} %multiply_multiply_fusion, f32[3,2,16,256]{3,2,1,0:T(8,128)S(1)} %fusion.6, pred[16,16]{1,0:T(8,128)(4,1)S(1)} %copy-done.14), kind=kOutput, calls=%fused_computation.34 | convolution fusion | flops 2416312320 | bytes 11108608 | tf_op jit(solution)/shard_map/ceabm,cmn->ceabn/dot_general | solution.py:136
  197.2 8.4 %reshape.1073 = f32[3,2,256,16,16]{4,3,2,1,0:T(8,128)} reshape(f32[3,2,16,16,256]{4,3,2,1,0:T(8,128)} %fusion.23) | data formatting | bytes 3145728 | tf_op jit(solution)/shard_map/reshape | solution.py:161
  205.6 9.3 %fusion.2 = f32[3,256,128,2,16]{2,4,3,1,0:T(8,128)} fusion(f32[3,2,256,16,16]{4,3,2,1,0:T(8,128)} %reshape.1073, pred[3,2,256,16,128]{4,3,2,0,1:T(8,128)(4,1)S(1)} %copy-done.2), kind=kOutput, calls=%fused_computation.2 | convolution fusion | flops 301989888 | bytes 15728640 | tf_op jit(solution)/shard_map/cekrt,cktw->ckrew/dot_general | solution.py:166
  214.9 9.8 %fusion = f32[3,2,128,128,1]{3,2,1,4,0:T(8,128)S(1)} fusion(f32[3,256,128,2,16]{2,4,3,1,0:T(8,128)} %fusion.2, pred[3,2,256,16,128]{4,3,2,0,1:T(8,128)(4,1)S(1)} %copy-done.2), kind=kOutput, calls=%fused_computation | convolution fusion | flops 2415919104 | bytes 14548992 | tf_op jit(solution)/shard_map/ckru,ckrew->ucew/dot_general | solution.py:167
  225.7 19.1 %reduce-scatter.2.cloned.1.call-done = f32[32,3,256]{2,0,1:T(8,128)} async-done(((f32[128,3,256]{2,0,1:T(8,128)}), f32[32,3,256]{2,0,1:T(8,128)}) %reduce-scatter.2.cloned.1.call-update) | async-done | bytes 98320 | tf_op jit(solution)/shard_map/reduce_scatter | solution.py:169
  (114 shorter events, 17.3 us)
Async XLA Ops:
  6.5 5.2 %copy-start = (f32[8,7]{1,0:T(8,128)S(1)}, f32[8,7]{1,0:T(8,128)}, u32[]{:S(2)}) copy-start(f32[8,7]{1,0:T(8,128)} %param.18) | copy-start | bytes 676
  6.5 6.3 %copy-start.12 = (f32[16,256,1]{1,0,2:T(8,128)S(1)}, f32[16,256,1]{1,0,2:T(8,128)}, u32[]{:S(2)}) copy-start(f32[16,256,1]{1,0,2:T(8,128)} %constant.175) | copy-start | bytes 49156
  6.5 6.5 %copy-start.9 = (f32[1024,9,1]{0,1,2:T(8,128)S(1)}, f32[1024,9,1]{0,1,2:T(8,128)}, u32[]{:S(2)}) copy-start(f32[1024,9,1]{0,1,2:T(8,128)} %constant.176) | copy-start | bytes 110596
  6.5 4.8 %copy-start.13 = (f32[16,48]{1,0:T(8,128)S(1)}, f32[16,48]{1,0:T(8,128)}, u32[]{:S(2)}) copy-start(f32[16,48]{1,0:T(8,128)} %param.15) | copy-start | bytes 9220
  6.5 5.9 %copy-start.15 = (s32[3,2,136]{2,1,0:T(2,128)S(1)}, s32[3,2,136]{2,1,0:T(2,128)}, u32[]{:S(2)}) copy-start(s32[3,2,136]{2,1,0:T(2,128)} %param.17) | copy-start | bytes 9796
  8.9 11.4 %collective-permute-start = (bf16[128,768]{1,0:T(8,128)(2,1)S(1)}, bf16[128,768]{1,0:T(8,128)(2,1)S(1)}, u32[]{:S(2)}, u32[]{:S(2)}) collective-permute-start(bf16[128,768]{1,0:T(8,128)(2,1)S(1)} %slice.169), channel_id=1, source_target_pairs={{0,1},{1,2},{2,3},{4,5},{5,6},{6,7},{8,9},{9,10},{10,11},{12,13},{... | collective-permute-start | bytes 589832 | tf_op jit(solution)/shard_map/ppermute | solution.py:18
  12.2 5.2 %copy-start.7 = (f32[136,256,1]{1,0,2:T(8,128)S(1)}, f32[136,256,1]{1,0,2:T(8,128)}, u32[]{:S(2)}) copy-start(f32[136,256,1]{1,0,2:T(8,128)} %constant.174) | copy-start | bytes 417796
  12.2 5.2 %copy-start.25 = (s32[256]{0:T(256)S(1)}, s32[256]{0:T(256)}, u32[]{:S(2)}) copy-start(s32[256]{0:T(256)} %constant.139.clone) | copy-start | bytes 3076
  12.7 5.5 %copy-start.17 = (f32[384]{0:T(512)S(1)}, f32[384]{0:T(512)}, u32[]{:S(2)}) copy-start(f32[384]{0:T(512)} %constant.173) | copy-start | bytes 4612
  12.7 5.5 %copy-start.18 = (f32[384]{0:T(512)S(1)}, f32[384]{0:T(512)}, u32[]{:S(2)}) copy-start(f32[384]{0:T(512)} %constant.171) | copy-start | bytes 4612
  12.7 5.5 %copy-start.19 = (f32[384]{0:T(512)S(1)}, f32[384]{0:T(512)}, u32[]{:S(2)}) copy-start(f32[384]{0:T(512)} %constant.169) | copy-start | bytes 4612
  12.7 5.5 %copy-start.20 = (f32[384]{0:T(512)S(1)}, f32[384]{0:T(512)}, u32[]{:S(2)}) copy-start(f32[384]{0:T(512)} %constant.167) | copy-start | bytes 4612
  12.7 5.5 %copy-start.21 = (f32[384]{0:T(512)S(1)}, f32[384]{0:T(512)}, u32[]{:S(2)}) copy-start(f32[384]{0:T(512)} %constant.165) | copy-start | bytes 4612
  12.7 5.5 %copy-start.22 = (f32[384]{0:T(512)S(1)}, f32[384]{0:T(512)}, u32[]{:S(2)}) copy-start(f32[384]{0:T(512)} %constant.163) | copy-start | bytes 4612
  12.7 5.5 %copy-start.23 = (f32[384]{0:T(512)S(1)}, f32[384]{0:T(512)}, u32[]{:S(2)}) copy-start(f32[384]{0:T(512)} %constant.161) | copy-start | bytes 4612
  12.8 5.4 %copy-start.24 = (f32[384]{0:T(512)S(1)}, f32[384]{0:T(512)}, u32[]{:S(2)}) copy-start(f32[384]{0:T(512)} %constant.159) | copy-start | bytes 4612
  13.1 6.5 %copy-start.11 = (f32[16,256,1]{1,0,2:T(8,128)S(1)}, f32[16,256,1]{1,0,2:T(8,128)}, u32[]{:S(2)}) copy-start(f32[16,256,1]{1,0,2:T(8,128)} %constant.177) | copy-start | bytes 49156
  83.2 2.6 %copy-start.3 = (bf16[8,3,2,64,128]{3,4,2,1,0:T(8,128)(2,1)S(1)}, bf16[8,3,2,64,128]{3,4,2,1,0:T(8,128)(2,1)}, u32[]{:S(2)}) copy-start(bf16[8,3,2,64,128]{3,4,2,1,0:T(8,128)(2,1)} %constant_dynamic-update-slice_fusion.9) | copy-start | bytes 2359300
  90.7 8.5 %copy-start.16 = (s32[2,512]{1,0:T(2,128)S(1)}, s32[2,512]{1,0:T(2,128)}, u32[]{:S(2)}) copy-start(s32[2,512]{1,0:T(2,128)} %param.16) | copy-start | bytes 12292
  90.7 8.6 %copy-start.10 = (s32[3,2,256]{2,0,1:T(4,128)S(1)}, s32[3,2,256]{2,0,1:T(4,128)}, u32[]{:S(2)}) copy-start(s32[3,2,256]{2,0,1:T(4,128)} %fusion.29) | copy-start | bytes 18436
  92.2 7.4 %copy-start.6 = (f32[3,9,256]{2,1,0:T(8,128)S(1)}, f32[3,9,256]{2,1,0:T(8,128)}, u32[]{:S(2)}) copy-start(f32[3,9,256]{2,1,0:T(8,128)} %fusion.52) | copy-start | bytes 82948
  92.2 7.4 %copy-start.8 = (f32[1024,9,1]{0,1,2:T(8,128)S(1)}, f32[1024,9,1]{0,1,2:T(8,128)}, u32[]{:S(2)}) copy-start(f32[1024,9,1]{0,1,2:T(8,128)} %constant.178) | copy-start | bytes 110596
  92.2 28.4 %all-to-all-start = ((bf16[8,3,2,64,128]{4,3,2,1,0:T(8,128)(2,1)}), bf16[8,3,2,64,128]{4,3,2,1,0:T(8,128)(2,1)}, u32[]{:S(2)}, u32[]{:S(2)}) async-start(bf16[8,3,2,64,128]{4,3,2,1,0:T(8,128)(2,1)} %copy.112), calls=%async_computation | async-start | bytes 1572864 | tf_op jit(solution)/shard_map/all_to_all | solution.py:109
  99.0 145.9 %reduce-scatter.2.cloned.1.call-start = ((), (), s32[]{:S(2)}) async-start(), calls=%async_computation.2 | async-start | bytes 491520 | tf_op jit(solution)/shard_map/reduce_scatter | solution.py:169
  178.4 1.6 copy-start.4
  178.4 1.6 copy-start.5
  178.4 1.6 copy-start.26
  188.8 1.6 copy-start.14
  197.2 8.4 %copy-start.2 = (pred[3,2,256,16,128]{4,3,2,0,1:T(8,128)(4,1)S(1)}, pred[3,2,256,16,128]{4,3,2,0,1:T(8,128)(4,1)}, u32[]{:S(2)}) copy-start(pred[3,2,256,16,128]{4,3,2,0,1:T(8,128)(4,1)} %iota_compare_fusion) | copy-start | bytes 9437188
  214.9 29.9 %copy-start.1 = (f32[8,7]{1,0:T(8,128)S(1)}, f32[8,7]{1,0:T(8,128)}, u32[]{:S(2)}) copy-start(f32[8,7]{1,0:T(8,128)} %param.18) | copy-start | bytes 676
Sparse Core Ops, SparseCore 0:
  225.9 18.9 reduce-scatter.1
